TPU v7x, 32 devices: a whole 2x2x4 slice. The times are simulated.
32 devices in a mesh: section: 8 (over y, x, core), dp: 4 (over z).
Axes of the slice: x: 2, y: 2, z: 4, core: 2. Of those that a mesh axis runs over, the one named last changes fastest.
Arguments:
- stash_q: bfloat16 [8, 4, 128, 4096], P('section', 'dp'), may hold values from -5.5 to 5.5
- stash_kv: bfloat16 [8, 4, 128, 1024], P('section', 'dp'), may hold values from -5.5 to 5.5
- upstream: bfloat16 [8, 4, 128, 4096], P('section', 'dp'), may hold values from -6 to 6
- lengths: int32 [4], P('dp'), may hold values from 2 to 128, as said below
- domains: int32 [4], P('dp'), may hold values from 0 to 6
- domain_weight: float32 [7], replicated, may hold values from 0.3 to 3
Outputs:
- grad_q: bfloat16 [8, 4, 128, 4096], P('section', 'dp')
- grad_kv: bfloat16 [8, 4, 128, 1024], P('section', 'dp')
Inputs may be any that keep to these rules, and one draw needn't show every extreme that they name: `lengths`: some micro-batch has exactly 128 live tokens.
All inputs are finite; a program needn't handle non-finite values.
Results may differ from a plain program's by a relative error of at most 0.006.
Values may be sent and summed in bfloat16 or wider, within the bound.
A program may use at most 64 MiB of HBM per device.

v0:
```python
import math

import jax
import jax.numpy as jnp
from jax import lax
from jax.sharding import PartitionSpec as P

QUERY_HEADS = 32
KEY_VALUE_HEADS = 4
HEAD_SIZE = 128
DOMAINS = 7


def shifted(array, axis, by):
    count = lax.axis_size(axis)
    return lax.ppermute(array, axis, [(i, (i + by) % count) for i in range(count)])


def swapped(array, axis, apart):
    return lax.ppermute(array, axis, [(i, i ^ 1 << apart) for i in range(lax.axis_size(axis))])


def backward_heads(query_rows, key_portion, value_portion, grads, lengths, kv_heads):
    batch_list = query_rows.shape[0]
    seq_len = query_rows.shape[1]
    head_dim = key_portion.shape[-1] // kv_heads
    group_count = query_rows.shape[-1] // (kv_heads * head_dim)
    inv_root = 1.0 / math.sqrt(head_dim)
    query_head_rows = query_rows.reshape(batch_list, seq_len, kv_heads, group_count, head_dim)
    key_head_rows = key_portion.reshape(batch_list, seq_len, kv_heads, head_dim)
    value_head_rows = value_portion.reshape(batch_list, seq_len, kv_heads, head_dim)
    row_index = jnp.arange(seq_len, dtype=jnp.int32)[:, None]
    col_index = jnp.arange(seq_len, dtype=jnp.int32)[None, :]
    allowed = (col_index <= row_index)[None] & (col_index[None] < lengths[:, None, None])
    live = jnp.arange(seq_len, dtype=jnp.int32)[None, :] < lengths[:, None]
    grad_masked = jnp.where(live[:, :, None], grads, jnp.zeros((), grads.dtype))
    gradient_heads = grad_masked.reshape(batch_list, seq_len, kv_heads, group_count, head_dim)
    scores = (
        jnp.einsum(
            "bikgd,bjkd->bkgij", query_head_rows, key_head_rows, preferred_element_type=jnp.float32
        )
        * inv_root
    )
    scores = jnp.where(allowed[:, None, None], scores, jnp.float32(-1e30))
    peak = jnp.max(scores, axis=-1, keepdims=True)
    expo = jnp.exp(scores - peak)
    probability = expo / jnp.sum(expo, axis=-1, keepdims=True)
    prob_half = probability.astype(jnp.bfloat16)
    value_gradient = jnp.einsum(
        "bkgij,bikgd->bjkd", prob_half, gradient_heads, preferred_element_type=jnp.float32
    )
    prob_grad = jnp.einsum(
        "bikgd,bjkd->bkgij", gradient_heads, value_head_rows, preferred_element_type=jnp.float32
    )
    row_total = jnp.sum(probability * prob_grad, axis=-1, keepdims=True)
    score_grad = (probability * (prob_grad - row_total) * inv_root).astype(jnp.bfloat16)
    query_grad = jnp.einsum(
        "bkgij,bjkd->bikgd", score_grad, key_head_rows, preferred_element_type=jnp.float32
    )
    key_gradient = jnp.einsum(
        "bkgij,bikgd->bjkd", score_grad, query_head_rows, preferred_element_type=jnp.float32
    )
    return (
        query_grad.reshape(batch_list, seq_len, kv_heads * group_count * head_dim),
        key_gradient.reshape(batch_list, seq_len, kv_heads * head_dim),
        value_gradient.reshape(batch_list, seq_len, kv_heads * head_dim),
    )


def body(stash_q, stash_kv, upstream, lengths, domains, domain_weight):
    section_bits = lax.axis_size("section").bit_length() - 1
    domain_ids = jnp.arange(DOMAINS, dtype=jnp.int32)
    onehot = domains[:, None] == domain_ids[None, :]
    partial_count = jnp.sum(jnp.where(onehot, lengths[:, None], 0), axis=0)
    counts = lax.psum(partial_count, "dp").astype(jnp.float32)
    token_total = jnp.sum(counts)
    own_count = jnp.sum(jnp.where(onehot, counts[None, :], jnp.float32(0.0)), axis=1)
    weight = jnp.sum(jnp.where(onehot, domain_weight[None, :], jnp.float32(0.0)), axis=1)
    factor = weight * token_total / (DOMAINS * own_count)
    next_grads = shifted(upstream, "section", -1)[0]
    key_span = KEY_VALUE_HEADS * HEAD_SIZE
    group_span = QUERY_HEADS // KEY_VALUE_HEADS * HEAD_SIZE
    query_list = []
    key_list = []
    value_list = []
    query_got, pair_got = swapped((stash_q, stash_kv), "section", section_bits - 1)
    query_all = query_got[0]
    pair_all = pair_got[0]
    for head_number in range(KEY_VALUE_HEADS):
        query_part = query_all[..., head_number * group_span : (head_number + 1) * group_span]
        key_part = pair_all[..., head_number * HEAD_SIZE : (head_number + 1) * HEAD_SIZE]
        value_part = pair_all[
            ..., key_span + head_number * HEAD_SIZE : key_span + (head_number + 1) * HEAD_SIZE
        ]
        grad_part = next_grads[..., head_number * group_span : (head_number + 1) * group_span]
        query_grad, key_gradient, value_gradient = backward_heads(
            query_part, key_part, value_part, grad_part, lengths, 1
        )
        query_list.append(query_grad)
        key_list.append(key_gradient)
        value_list.append(value_gradient)
    query_grad = jnp.concatenate(query_list, axis=-1)
    key_gradient = jnp.concatenate(key_list, axis=-1)
    value_gradient = jnp.concatenate(value_list, axis=-1)
    row_scales = factor[:, None, None]
    out_q = (query_grad * row_scales).astype(jnp.bfloat16)
    out_kv = jnp.concatenate(
        [key_gradient * row_scales, value_gradient * row_scales], axis=-1
    ).astype(jnp.bfloat16)
    return (out_q[None], out_kv[None])


def solution(mesh):
    return jax.shard_map(
        body,
        mesh=mesh,
        in_specs=(
            P("section", "dp", None, None),
            P("section", "dp", None, None),
            P("section", "dp", None, None),
            P("dp"),
            P("dp"),
            P(),
        ),
        out_specs=(P("section", "dp", None, None), P("section", "dp", None, None)),
        check_vma=False,
    )
```

profile of v0, /device:TPU:7, one launch (start us, length us, event | category | flops | bytes accessed | tf_op | source)
XLA Modules:
  0.0 60.3 jit_solution(4005914009554279289)
XLA Ops:
  0.6 0.7 %collective-permute-start.2 = (bf16[1,1,128,4096]{3,2,1,0:T(8,128)(2,1)}, bf16[1,1,128,4096]{3,2,1,0:T(8,128)(2,1)S(1)}, u32[]{:S(2)}, u32[]{:S(2)}) collective-permute-start(bf16[1,1,128,4096]{3,2,1,0:T(8,128)(2,1)} %param.8), channel_id=1, source_target_pairs={{0,28},{4,0},{8,4},{12,8},{16,12},{20,16},{24,20},{28,24},{1,29},{... | collective-permute-start | bytes 3145736 | tf_op jit(solution)/shard_map/ppermute | solution.py:16
  1.4 1.6 %copy.41 = bf16[1,1,128,4096]{2,3,1,0:T(8,128)(2,1)S(1)} copy(bf16[1,1,128,4096]{3,2,1,0:T(8,128)(2,1)} %param.6) | data formatting | bytes 2097152 | tf_op args[0]
  3.0 0.3 collective-permute-start.1
  4.6 1.3 %collective-permute-start = (bf16[1,1,128,1024]{3,2,1,0:T(8,128)(2,1)}, bf16[1,1,128,1024]{3,2,1,0:T(8,128)(2,1)S(1)}, u32[]{:S(2)}, u32[]{:S(2)}) collective-permute-start(bf16[1,1,128,1024]{3,2,1,0:T(8,128)(2,1)} %param.7), channel_id=1, source_target_pairs={{0,16},{4,20},{8,24},{12,28},{16,0},{20,4},{24,8},{28,12},{1,17},{... | collective-permute-start | bytes 786440 | tf_op jit(solution)/shard_map/ppermute | solution.py:20
  5.9 6.7 %psum.7 = s32[7]{0:T(128)S(1)} all-reduce(s32[7]{0:T(128)S(1)} %fusion.38), channel_id=1, replica_groups=mesh['section'=8,'dp'=4] {'dp'}, use_global_device_ids=true, to_apply=%region_13.14 | all-reduce | flops 7 | bytes 56 | tf_op jit(solution)/shard_map/psum | solution.py:75
  12.6 0.7 %select_reduce_fusion.1 = f32[]{:T(128)} fusion(f32[7]{0:T(128)S(1)} %copy-done.12, s32[]{:T(128)} %bitcast.279), kind=kLoop, calls=%fused_computation.89 | loop fusion | flops 20 | bytes 36 | tf_op jit(solution)/shard_map/reduce_sum | solution.py:78
  13.3 0.6 %select_reduce_fusion = (f32[]{:T(128)}, f32[]{:T(128)}) fusion(s32[7]{0:T(128)S(1)} %psum.7, s32[]{:T(128)} %bitcast.281), kind=kLoop, calls=%fused_computation.87 | loop fusion | flops 33 | bytes 40 | tf_op jit(solution)/shard_map/reduce_sum | solution.py:77
  16.3 22.4 %collective-permute-done.1 = bf16[1,1,128,4096]{2,3,1,0:T(8,128)(2,1)S(1)} collective-permute-done((bf16[1,1,128,4096]{2,3,1,0:T(8,128)(2,1)S(1)}, bf16[1,1,128,4096]{2,3,1,0:T(8,128)(2,1)S(1)}, u32[]{:S(2)}, u32[]{:S(2)}) %collective-permute-start.1) | collective-permute-done | bytes 1048608 | tf_op jit(solution)/shard_map/ppermute | solution.py:20
  38.8 5.5 %collective-permute-done = bf16[1,1,128,1024]{3,2,1,0:T(8,128)(2,1)S(1)} collective-permute-done((bf16[1,1,128,1024]{3,2,1,0:T(8,128)(2,1)}, bf16[1,1,128,1024]{3,2,1,0:T(8,128)(2,1)S(1)}, u32[]{:S(2)}, u32[]{:S(2)}) %collective-permute-start) | collective-permute-done | bytes 262176 | tf_op jit(solution)/shard_map/ppermute | solution.py:20
  44.7 0.2 multiply_reduce_fusion.3
  45.4 0.3 fusion.34
  45.7 0.2 fusion.42
  46.0 0.2 multiply_reduce_fusion.2
  46.3 0.3 copy-done.1
  46.8 0.2 convolution_bitcast_fusion.10
  47.1 0.3 fusion.35
  47.3 0.2 fusion.41
  47.7 0.2 multiply_reduce_fusion.1
  48.0 0.3 copy-done.3
  48.5 0.9 %convolution_bitcast_fusion.9 = f32[128,128]{0,1:T(8,128)} fusion(bf16[8,128,128]{1,2,0:T(8,128)(2,1)S(1)} %get-tuple-element.21, bf16[128,8,128]{0,2,1:T(8,128)(2,1)S(1)} %bitcast.285), kind=kOutput, calls=%fused_computation.23 | convolution fusion | flops 33554432 | bytes 589824 | tf_op jit(solution)/shard_map/bkgij,bikgd->bjkd/dot_general | solution.py:60
  49.4 0.3 fusion.36
  50.0 0.2 multiply_reduce_fusion
  50.3 0.3 copy-done.5
  50.8 0.9 %convolution_bitcast_fusion.8 = f32[128,128]{0,1:T(8,128)} fusion(bf16[8,128,128]{1,2,0:T(8,128)(2,1)S(1)} %get-tuple-element.23, bf16[128,8,128]{0,2,1:T(8,128)(2,1)S(1)} %bitcast.283), kind=kOutput, calls=%fused_computation.22 | convolution fusion | flops 33554432 | bytes 589824 | tf_op jit(solution)/shard_map/bkgij,bikgd->bjkd/dot_general | solution.py:60
  51.7 0.3 fusion.37
  52.1 1.9 %convolution_bitcast_fusion.7 = f32[128,128]{0,1:T(8,128)} fusion(bf16[128,8,128]{2,1,0:T(8,128)(2,1)} %bitcast.309, bf16[8,128,128]{2,0,1:T(8,128)(2,1)S(1)} %copy.92), kind=kOutput, calls=%fused_computation.21 | convolution fusion | flops 33554432 | bytes 589824 | tf_op jit(solution)/shard_map/bkgij,bikgd->bjkd/dot_general | solution.py:49
  54.2 0.9 %convolution_bitcast_fusion.6 = f32[128,128]{0,1:T(8,128)} fusion(bf16[128,8,128]{2,1,0:T(8,128)(2,1)S(1)} %bitcast.311, bf16[8,128,128]{2,0,1:T(8,128)(2,1)S(1)} %copy.94), kind=kOutput, calls=%fused_computation.20 | convolution fusion | flops 33554432 | bytes 589824 | tf_op jit(solution)/shard_map/bkgij,bikgd->bjkd/dot_general | solution.py:49
  55.4 0.9 %convolution_bitcast_fusion.5 = f32[128,128]{0,1:T(8,128)} fusion(bf16[128,8,128]{2,1,0:T(8,128)(2,1)S(1)} %bitcast.313, bf16[8,128,128]{2,0,1:T(8,128)(2,1)S(1)} %copy.96), kind=kOutput, calls=%fused_computation.19 | convolution fusion | flops 33554432 | bytes 589824 | tf_op jit(solution)/shard_map/bkgij,bikgd->bjkd/dot_general | solution.py:49
  56.5 0.3 convolution_bitcast_fusion.4
  56.8 0.5 copy-done.7
  57.5 0.9 %copy.74 = bf16[1,1,128,1024]{3,2,1,0:T(8,128)(2,1)} copy(bf16[1,1,128,1024]{2,3,1,0:T(8,128)(2,1)S(1)} %pad_maximum_fusion) | data formatting | bytes 524288
  59.2 1.1 %fusion = bf16[1,1,128,4096]{3,2,1,0:T(8,128)(2,1)} fusion(f32[1,1,128,1024]{3,2,1,0:T(8,128)S(1)} %copy.61, f32[1,1,128,1024]{3,2,1,0:T(8,128)S(1)} %copy.60, f32[1,1,128,1024]{3,2,1,0:T(8,128)S(1)} %copy.59, f32[1,1,128,1024]{3,2,1,0:T(8,128)S(1)} %copy.58, f32[]{:T(128)S(6)} %div.44), kind=kLoop, calls=%fused_computation.1 | loop fusion | flops 2621440 | bytes 3145732 | tf_op jit(solution)/shard_map/convert_element_type | solution.py:106
  (53 shorter events, 4.2 us)
Async XLA Ops:
  0.6 12.0 %copy-start.12 = (f32[7]{0:T(128)S(1)}, f32[7]{0:T(128)}, u32[]{:S(2)}) copy-start(f32[7]{0:T(128)} %param.11) | copy-start | bytes 88
  0.6 15.5 %collective-permute-start.2 = (bf16[1,1,128,4096]{3,2,1,0:T(8,128)(2,1)}, bf16[1,1,128,4096]{3,2,1,0:T(8,128)(2,1)S(1)}, u32[]{:S(2)}, u32[]{:S(2)}) collective-permute-start(bf16[1,1,128,4096]{3,2,1,0:T(8,128)(2,1)} %param.8), channel_id=1, source_target_pairs={{0,28},{4,0},{8,4},{12,8},{16,12},{20,16},{24,20},{28,24},{1,29},{... | collective-permute-start | bytes 3145736 | tf_op jit(solution)/shard_map/ppermute | solution.py:16
  3.0 35.8 %collective-permute-start.1 = (bf16[1,1,128,4096]{2,3,1,0:T(8,128)(2,1)S(1)}, bf16[1,1,128,4096]{2,3,1,0:T(8,128)(2,1)S(1)}, u32[]{:S(2)}, u32[]{:S(2)}) collective-permute-start(bf16[1,1,128,4096]{2,3,1,0:T(8,128)(2,1)S(1)} %copy.41), channel_id=1, source_target_pairs={{0,16},{4,20},{8,24},{12,28},{16,0},{20,4},{24,8},{28,12},{1,17},{... | collective-permute-start | bytes 3145736 | tf_op jit(solution)/shard_map/ppermute | solution.py:20
  4.6 39.8 %collective-permute-start = (bf16[1,1,128,1024]{3,2,1,0:T(8,128)(2,1)}, bf16[1,1,128,1024]{3,2,1,0:T(8,128)(2,1)S(1)}, u32[]{:S(2)}, u32[]{:S(2)}) collective-permute-start(bf16[1,1,128,1024]{3,2,1,0:T(8,128)(2,1)} %param.7), channel_id=1, source_target_pairs={{0,16},{4,20},{8,24},{12,28},{16,0},{20,4},{24,8},{28,12},{1,17},{... | collective-permute-start | bytes 786440 | tf_op jit(solution)/shard_map/ppermute | solution.py:20
  16.3 28.6 %copy-start = (bf16[16,8,8,128]{3,2,1,0:T(8,128)(2,1)}, bf16[16,8,8,128]{3,2,1,0:T(8,128)(2,1)S(1)}, u32[]{:S(2)}) copy-start(bf16[16,8,8,128]{3,2,1,0:T(8,128)(2,1)S(1)} %copy.107) | copy-start | bytes 786436
  45.9 0.7 %copy-start.1 = (bf16[16,8,8,128]{3,2,1,0:T(8,128)(2,1)}, bf16[16,8,8,128]{3,2,1,0:T(8,128)(2,1)S(1)}, u32[]{:S(2)}) copy-start(bf16[16,8,8,128]{3,2,1,0:T(8,128)(2,1)S(1)} %copy.108) | copy-start | bytes 786436
  47.6 0.7 %copy-start.3 = (bf16[16,8,8,128]{3,2,1,0:T(8,128)(2,1)}, bf16[16,8,8,128]{3,2,1,0:T(8,128)(2,1)S(1)}, u32[]{:S(2)}) copy-start(bf16[16,8,8,128]{3,2,1,0:T(8,128)(2,1)S(1)} %copy.109) | copy-start | bytes 786436
  49.9 0.7 %copy-start.5 = (bf16[16,8,8,128]{3,2,1,0:T(8,128)(2,1)}, bf16[16,8,8,128]{3,2,1,0:T(8,128)(2,1)S(1)}, u32[]{:S(2)}) copy-start(bf16[16,8,8,128]{3,2,1,0:T(8,128)(2,1)S(1)} %copy.110) | copy-start | bytes 786436
  52.1 2.1 %copy-start.2 = (bf16[16,8,8,128]{3,2,1,0:T(8,128)(2,1)S(1)}, bf16[16,8,8,128]{3,2,1,0:T(8,128)(2,1)}, u32[]{:S(2)}) copy-start(bf16[16,8,8,128]{3,2,1,0:T(8,128)(2,1)} %copy-done.1) | copy-start | bytes 786436
  54.2 1.1 %copy-start.4 = (bf16[16,8,8,128]{3,2,1,0:T(8,128)(2,1)S(1)}, bf16[16,8,8,128]{3,2,1,0:T(8,128)(2,1)}, u32[]{:S(2)}) copy-start(bf16[16,8,8,128]{3,2,1,0:T(8,128)(2,1)} %copy-done.3) | copy-start | bytes 786436
  55.3 1.1 %copy-start.6 = (bf16[16,8,8,128]{3,2,1,0:T(8,128)(2,1)S(1)}, bf16[16,8,8,128]{3,2,1,0:T(8,128)(2,1)}, u32[]{:S(2)}) copy-start(bf16[16,8,8,128]{3,2,1,0:T(8,128)(2,1)} %copy-done.5) | copy-start | bytes 786436
  56.5 0.8 %copy-start.7 = (f32[128,128]{0,1:T(8,128)S(1)}, f32[128,128]{0,1:T(8,128)}, u32[]{:S(2)}) copy-start(f32[128,128]{0,1:T(8,128)} %convolution_bitcast_fusion.9) | copy-start | bytes 196612
  56.5 0.9 %copy-start.8 = (f32[128,128]{0,1:T(8,128)S(1)}, f32[128,128]{0,1:T(8,128)}, u32[]{:S(2)}) copy-start(f32[128,128]{0,1:T(8,128)} %convolution_bitcast_fusion.8) | copy-start | bytes 196612
  56.5 0.9 %copy-start.9 = (f32[128,128]{0,1:T(8,128)S(1)}, f32[128,128]{0,1:T(8,128)}, u32[]{:S(2)}) copy-start(f32[128,128]{0,1:T(8,128)} %convolution_bitcast_fusion.7) | copy-start | bytes 196612
  56.5 0.9 %copy-start.10 = (f32[128,128]{0,1:T(8,128)S(1)}, f32[128,128]{0,1:T(8,128)}, u32[]{:S(2)}) copy-start(f32[128,128]{0,1:T(8,128)} %convolution_bitcast_fusion.6) | copy-start | bytes 196612
  56.5 0.9 %copy-start.11 = (f32[128,128]{0,1:T(8,128)S(1)}, f32[128,128]{0,1:T(8,128)}, u32[]{:S(2)}) copy-start(f32[128,128]{0,1:T(8,128)} %convolution_bitcast_fusion.5) | copy-start | bytes 196612
where the time goes:
time: 60.6 us; the launch traced here: 60.3 us
  waiting for transfers between devices  28.1 us (46%)
  matrix products  9.06 us (15%)
  blocking collectives  6.72 us (11%)
  local copies, waits for them, and re-layouts  5.96 us (10%)
  between operations  4.31 us (7%)
  other arithmetic  3.8 us (6%)
  starting transfers between devices  2.32 us (4%)
    ppermute x2, waiting for transfers between devices, swapped(): lax.ppermute(array, axis, [(i, i ^ 1 << apart) for i in range(lax.axis_si...  28 us
    psum x1, blocking collectives, body(): counts = lax.psum(partial_count, 'dp').astype(jnp.float32)  6.72 us
    unnamed x32, local copies, waits for them, and re-layouts  4.36 us
    dot_general x4, matrix products, backward_heads(): jnp.einsum('bkgij,bikgd->bjkd', prob_half, gradient_heads, preferred_elem...  3.97 us
    dot_general x4, matrix products, backward_heads(): jnp.einsum('bkgij,bikgd->bjkd', score_grad, query_head_rows, preferred_el...  2.15 us
    ppermute x2, starting transfers between devices, swapped(): lax.ppermute(array, axis, [(i, i ^ 1 << apart) for i in range(lax.axis_si...  1.6 us
  transfers between devices with their start and end apart: 3, of which 3 were waited for; matrix products, arithmetic and copies ran while one was open for 5% of the time, Pallas kernels for 0%

commit v1 on v0

v1 whole, which is shorter than its diff:
```python
import functools
import math

import jax
import jax.numpy as jnp
from jax import lax
from jax.experimental import pallas as pl
from jax.experimental.pallas import tpu as pltpu
from jax.sharding import PartitionSpec as P

HEAD_SIZE = 128
DOMAINS = 7
MESH = pl.DeviceIdType.MESH
CHUNK_HEADS = 4
NT = (((1,), (1,)), ((), ()))
TN = (((0,), (0,)), ((), ()))


def kernel(n, replicas, len_ref, dom_ref, weight_ref, q_hbm, kv_hbm, g_hbm, dq_out, dkv_out,
           q_v, kv_v, g_v, dq_s, dkv_s, counts,
           q_send, q_recv, g_send, g_recv, kv_send, kv_recv, c_send, c_recv,
           dq_send, dq_recv, dkv_send, dkv_recv):
    seq, q_cols = q_v.shape
    span = kv_v.shape[1] // 2
    kv_heads = span // HEAD_SIZE
    group = q_cols // span
    width = min(CHUNK_HEADS, group) * HEAD_SIZE
    chunks = q_cols // width
    per_group = chunks // kv_heads
    inv_root = 1.0 / math.sqrt(HEAD_SIZE)

    me = lax.axis_index("section")
    replica = lax.axis_index("dp")
    half = n // 2
    pair = lax.rem(me + half, n)
    base = lax.div(me, half) * half
    place = me - base
    g_to = base + lax.rem(place + half - 1, half)
    g_from = base + lax.rem(place + 1, half)
    crossed = place == half - 1

    barrier = pltpu.get_barrier_semaphore()
    for other in (pair, g_to, g_from):
        pl.semaphore_signal(barrier, inc=1, device_id={"section": other}, device_id_type=MESH)
    for off in range(1, replicas):
        pl.semaphore_signal(barrier, inc=1, device_id={"dp": lax.rem(replica + off, replicas)},
                            device_id_type=MESH)

    length = len_ref[0]
    domain = dom_ref[0]
    lane = lax.broadcasted_iota(jnp.int32, (8, 128), 1)
    onehot = lane == domain
    counts[0] = jnp.where(onehot, length, 0)

    def cols(c):
        return pl.ds(pl.multiple_of(c * width, width), width)

    def remote(src, dst, send, recv, **to):
        return pltpu.make_async_remote_copy(src_ref=src, dst_ref=dst, send_sem=send, recv_sem=recv,
                                            device_id=to, device_id_type=MESH)

    def q_copy(c):
        return remote(q_hbm.at[0, 0, :, cols(c)], q_v.at[:, cols(c)], q_send.at[c], q_recv.at[c],
                      section=pair)

    def q_local(c):
        return pltpu.make_async_copy(q_hbm.at[0, 0, :, cols(c)], q_v.at[:, cols(c)], q_recv.at[c])

    def g_copy(c):
        return remote(g_hbm.at[0, 0, :, cols(c)], g_v.at[:, cols(c)], g_send.at[c], g_recv.at[c],
                      section=g_to)

    def dq_copy(c):
        return remote(dq_s.at[:, cols(c)], dq_out.at[0, 0, :, cols(c)], dq_send.at[c], dq_recv.at[c],
                      section=pair)

    def dq_local(c):
        return pltpu.make_async_copy(dq_s.at[:, cols(c)], dq_out.at[0, 0, :, cols(c)], dq_send.at[c])

    kv_copy = remote(kv_hbm.at[0, 0], kv_v, kv_send, kv_recv, section=pair)
    kv_local = pltpu.make_async_copy(kv_hbm.at[0, 0], kv_v, kv_recv)
    dkv_copy = remote(dkv_s, dkv_out.at[0, 0], dkv_send, dkv_recv, section=pair)
    dkv_local = pltpu.make_async_copy(dkv_s, dkv_out.at[0, 0], dkv_send)
    count_copies = [
        remote(counts.at[0], counts.at[off], c_send.at[off], c_recv.at[off],
               dp=lax.rem(replica + off, replicas))
        for off in range(1, replicas)
    ]

    @pl.when(crossed)
    def _():
        kv_local.start()
        for c in range(chunks):
            q_local(c).start()

    pl.semaphore_wait(barrier, 3 + replicas - 1)

    @pl.when(jnp.logical_not(crossed))
    def _():
        kv_copy.start()

    for copy in count_copies:
        copy.start()
    for c in range(chunks):
        g_copy(c).start()

        @pl.when(jnp.logical_not(crossed))
        def _():
            q_copy(c).start()

    weight = jnp.float32(0.0)
    for d in range(DOMAINS):
        weight = jnp.where(domain == d, weight_ref[d], weight)
    for copy in count_copies:
        copy.wait()
    total = counts[0, 0:1]
    for off in range(1, replicas):
        total = total + counts[off, 0:1]
    total = total.astype(jnp.float32)
    own = jnp.sum(jnp.where(onehot[0:1], total, 0.0), axis=1, keepdims=True)
    factor = weight * jnp.sum(total, axis=1, keepdims=True) / (DOMAINS * own)

    key_row = lax.broadcasted_iota(jnp.int32, (seq, seq), 0)
    query_col = lax.broadcasted_iota(jnp.int32, (seq, seq), 1)
    allowed = (key_row <= query_col) & (key_row < length)
    live = query_col[0:1] < length

    @pl.when(crossed)
    def _():
        kv_local.wait()

    @pl.when(jnp.logical_not(crossed))
    def _():
        kv_copy.wait_recv()

    def one_group(k, carry):
        at_k = pl.ds(pl.multiple_of(k * HEAD_SIZE, HEAD_SIZE), HEAD_SIZE)
        at_v = pl.ds(pl.multiple_of(span + k * HEAD_SIZE, HEAD_SIZE), HEAD_SIZE)
        key = kv_v[:, at_k]
        value = kv_v[:, at_v]
        d_key = jnp.zeros((seq, HEAD_SIZE), jnp.float32)
        d_value = jnp.zeros((seq, HEAD_SIZE), jnp.float32)
        for sub in range(per_group):
            c = k * per_group + sub
            g_copy(c).wait_recv()

            @pl.when(crossed)
            def _():
                q_local(c).wait()

            @pl.when(jnp.logical_not(crossed))
            def _():
                q_copy(c).wait_recv()

            for h in range(width // HEAD_SIZE):
                at = pl.ds(pl.multiple_of(c * width + h * HEAD_SIZE, HEAD_SIZE), HEAD_SIZE)
                query = q_v[:, at]
                grad = g_v[:, at]
                scores = lax.dot_general(key, query, NT, preferred_element_type=jnp.float32)
                scores = jnp.where(allowed, scores, -1e30)
                peak = jnp.max(scores, axis=0, keepdims=True)
                expo = jnp.exp2((scores - peak) * (inv_root * math.log2(math.e)))
                scale = jnp.where(live, 1.0 / jnp.sum(expo, axis=0, keepdims=True), 0.0)
                prob = expo * scale
                d_prob = lax.dot_general(value, grad, NT, preferred_element_type=jnp.float32)
                row_total = jnp.sum(prob * d_prob, axis=0, keepdims=True)
                d_scores = (prob * (d_prob - row_total) * inv_root).astype(jnp.bfloat16)
                d_value += jnp.dot(prob.astype(jnp.bfloat16), grad, preferred_element_type=jnp.float32)
                d_key += jnp.dot(d_scores, query, preferred_element_type=jnp.float32)
                d_query = lax.dot_general(d_scores, key, TN, preferred_element_type=jnp.float32)
                dq_s[:, at] = (d_query * factor).astype(dq_s.dtype)

            @pl.when(crossed)
            def _():
                dq_copy(c).start()

            @pl.when(jnp.logical_not(crossed))
            def _():
                dq_local(c).start()

        dkv_s[:, at_k] = (d_key * factor).astype(dkv_s.dtype)
        dkv_s[:, at_v] = (d_value * factor).astype(dkv_s.dtype)
        return carry

    lax.fori_loop(0, kv_heads, one_group, 0)

    @pl.when(crossed)
    def _():
        dkv_copy.start()
        for c in range(chunks):
            dq_copy(c).wait()
        dkv_copy.wait()

    @pl.when(jnp.logical_not(crossed))
    def _():
        dkv_local.start()
        kv_copy.wait_send()
        for c in range(chunks):
            q_copy(c).wait_send()
            dq_local(c).wait()
        dkv_local.wait()

    for c in range(chunks):
        g_copy(c).wait_send()


def body(n, replicas, stash_q, stash_kv, upstream, lengths, domains, domain_weight):
    _, _, seq, q_cols = stash_q.shape
    kv_cols = stash_kv.shape[-1]
    group = 2 * q_cols // kv_cols
    chunks = q_cols // (min(CHUNK_HEADS, group) * HEAD_SIZE)
    dma = pltpu.SemaphoreType.DMA
    flops = 5 * 2 * seq * seq * q_cols
    return pl.pallas_call(
        functools.partial(kernel, n, replicas),
        out_shape=(
            jax.ShapeDtypeStruct(stash_q.shape, stash_q.dtype),
            jax.ShapeDtypeStruct(stash_kv.shape, stash_kv.dtype),
        ),
        in_specs=[pl.BlockSpec(memory_space=pltpu.SMEM)] * 3 + [pl.BlockSpec(memory_space=pltpu.HBM)] * 3,
        out_specs=[pl.BlockSpec(memory_space=pl.ANY)] * 2,
        scratch_shapes=[
            pltpu.VMEM((seq, q_cols), jnp.bfloat16),
            pltpu.VMEM((seq, kv_cols), jnp.bfloat16),
            pltpu.VMEM((seq, q_cols), jnp.bfloat16),
            pltpu.VMEM((seq, q_cols), jnp.bfloat16),
            pltpu.VMEM((seq, kv_cols), jnp.bfloat16),
            pltpu.VMEM((replicas, 8, 128), jnp.int32),
            dma((chunks,)), dma((chunks,)), dma((chunks,)), dma((chunks,)),
            dma, dma, dma((replicas,)), dma((replicas,)),
            dma((chunks,)), dma((chunks,)), dma, dma,
        ],
        compiler_params=pltpu.CompilerParams(
            collective_id=0, has_side_effects=True, vmem_limit_bytes=24 * 1024 * 1024
        ),
        cost_estimate=pl.CostEstimate(flops=flops, bytes_accessed=4 * 2 * seq * q_cols, transcendentals=seq * q_cols),
    )(lengths, domains, domain_weight, stash_q, stash_kv, upstream)


def solution(mesh):
    spec = P("section", "dp", None, None)
    return jax.shard_map(
        functools.partial(body, mesh.shape["section"], mesh.shape["dp"]),
        mesh=mesh,
        in_specs=(spec, spec, spec, P("dp"), P("dp"), P()),
        out_specs=(spec, spec),
        check_vma=False,
    )
```

time: 60.6 us -> 44.8 us (0.74)
  the two profiles are of different devices: /device:TPU:7 before, /device:TPU:0 now
where the time goes in v1:
time: 44.8 us; the launch traced here: 44.5 us
  Pallas kernels  37.5 us (84%)
  local copies, waits for them, and re-layouts  5.07 us (11%)
  between operations  1.97 us (4%)
    pallas_call x1, Pallas kernels, body(): pl.pallas_call(functools.partial(kernel, n, replicas), out_shape=(jax.Sha...  37.5 us
    unnamed x10, local copies, waits for them, and re-layouts  5.07 us

profile of v1, /device:TPU:0, one launch (start us, length us, event | category | flops | bytes accessed | tf_op | source)
XLA Modules:
  0.0 44.5 jit_solution(10177663592031498950)
XLA Ops:
  1.3 0.0 copy-start.3
  1.9 0.0 copy-done.3
  2.0 0.0 copy-start
  2.0 1.2 %copy-done = bf16[1,1,128,4096]{3,2,1,0:T(8,128)(2,1)S(1)} copy-done((bf16[1,1,128,4096]{3,2,1,0:T(8,128)(2,1)S(1)}, bf16[1,1,128,4096]{3,2,1,0:T(8,128)(2,1)}, u32[]{:S(2)}) %copy-start) | copy-done | bytes 1048600
  3.2 0.0 copy-start.1
  3.2 1.2 %copy-done.1 = bf16[1,1,128,4096]{3,2,1,0:T(8,128)(2,1)S(1)} copy-done((bf16[1,1,128,4096]{3,2,1,0:T(8,128)(2,1)S(1)}, bf16[1,1,128,4096]{3,2,1,0:T(8,128)(2,1)}, u32[]{:S(2)}) %copy-start.1) | copy-done | bytes 1048600
  4.4 0.0 copy-start.2
  4.4 0.9 %copy-done.2 = bf16[1,1,128,1024]{3,2,1,0:T(8,128)(2,1)S(1)} copy-done((bf16[1,1,128,1024]{3,2,1,0:T(8,128)(2,1)S(1)}, bf16[1,1,128,1024]{3,2,1,0:T(8,128)(2,1)}, u32[]{:S(2)}) %copy-start.2) | copy-done | bytes 262168
  5.4 37.5 %shard_map.77 = (bf16[1,1,128,4096]{3,2,1,0:T(8,128)(2,1)S(1)}, bf16[1,1,128,1024]{3,2,1,0:T(8,128)(2,1)S(1)}) custom-call(s32[1]{0:T(128)S(6)} %copy.10.len_ref, s32[1]{0:T(128)S(6)} %copy.11.dom_ref, f32[7]{0:T(128)S(1)} %copy-done.3, bf16[1,1,128,4096]{3,2,1,0:T(8,128)(2,1)S(1)} %copy-done, bf16[1,1,128,1024]{3,2,1,0:T(8,128)(2,1)S(1)} %copy-done.2, ...), custom_call_target="tpu_custom_call" | custom-call | flops 671088640 | bytes 4194304 | tf_op jit(solution)/shard_map/pallas_call | solution.py:214
  42.8 1.0 %copy.12 = bf16[1,1,128,4096]{3,2,1,0:T(8,128)(2,1)} copy(bf16[1,1,128,4096]{3,2,1,0:T(8,128)(2,1)S(1)} %get-tuple-element.4) | data formatting | bytes 2097152
  43.8 0.7 %copy.13 = bf16[1,1,128,1024]{3,2,1,0:T(8,128)(2,1)} copy(bf16[1,1,128,1024]{3,2,1,0:T(8,128)(2,1)S(1)} %get-tuple-element.5) | data formatting | bytes 524288
Async XLA Ops:
  1.3 0.7 %copy-start.3 = (f32[7]{0:T(128)S(1)}, f32[7]{0:T(128)}, u32[]{:S(2)}) copy-start(f32[7]{0:T(128)} %weight_ref.1) | copy-start | bytes 88
  2.0 1.2 %copy-start = (bf16[1,1,128,4096]{3,2,1,0:T(8,128)(2,1)S(1)}, bf16[1,1,128,4096]{3,2,1,0:T(8,128)(2,1)}, u32[]{:S(2)}) copy-start(bf16[1,1,128,4096]{3,2,1,0:T(8,128)(2,1)} %q_hbm.1) | copy-start | bytes 3145732
  3.2 1.2 %copy-start.1 = (bf16[1,1,128,4096]{3,2,1,0:T(8,128)(2,1)S(1)}, bf16[1,1,128,4096]{3,2,1,0:T(8,128)(2,1)}, u32[]{:S(2)}) copy-start(bf16[1,1,128,4096]{3,2,1,0:T(8,128)(2,1)} %g_hbm.1) | copy-start | bytes 3145732
  4.4 0.9 %copy-start.2 = (bf16[1,1,128,1024]{3,2,1,0:T(8,128)(2,1)S(1)}, bf16[1,1,128,1024]{3,2,1,0:T(8,128)(2,1)}, u32[]{:S(2)}) copy-start(bf16[1,1,128,1024]{3,2,1,0:T(8,128)(2,1)} %kv_hbm.1) | copy-start | bytes 786436

commit v2 on v1

--- a/solution.py
+++ b/solution.py
@@ -16,8 +16,8 @@
 TN = (((0,), (0,)), ((), ()))
 
 
-def kernel(n, replicas, len_ref, dom_ref, weight_ref, q_hbm, kv_hbm, g_hbm, dq_out, dkv_out,
-           q_v, kv_v, g_v, dq_s, dkv_s, counts,
+def kernel(n, replicas, len_hbm, dom_hbm, weight_hbm, q_hbm, kv_hbm, g_hbm, dq_out, dkv_out,
+           q_v, kv_v, g_v, dq_s, dkv_s, counts, len_ref, dom_ref, weight_ref, scalar_sems,
            q_send, q_recv, g_send, g_recv, kv_send, kv_recv, c_send, c_recv,
            dq_send, dq_recv, dkv_send, dkv_recv):
     seq, q_cols = q_v.shape
@@ -39,6 +39,13 @@
     g_from = base + lax.rem(place + 1, half)
     crossed = place == half - 1
 
+    scalars = [
+        pltpu.make_async_copy(src, dst, scalar_sems.at[i])
+        for i, (src, dst) in enumerate(
+            ((len_hbm, len_ref), (dom_hbm, dom_ref), (weight_hbm, weight_ref)))
+    ]
+    for copy in scalars:
+        copy.start()
     barrier = pltpu.get_barrier_semaphore()
     for other in (pair, g_to, g_from):
         pl.semaphore_signal(barrier, inc=1, device_id={"section": other}, device_id_type=MESH)
@@ -46,6 +53,8 @@
         pl.semaphore_signal(barrier, inc=1, device_id={"dp": lax.rem(replica + off, replicas)},
                             device_id_type=MESH)
 
+    for copy in scalars:
+        copy.wait()
     length = len_ref[0]
     domain = dom_ref[0]
     lane = lax.broadcasted_iota(jnp.int32, (8, 128), 1)
@@ -204,6 +213,14 @@
         g_copy(c).wait_send()
 
 
+def store(dq_in, dkv_in, dq_out, dkv_out, sems):
+    copies = [pltpu.make_async_copy(dq_in, dq_out, sems.at[0]), pltpu.make_async_copy(dkv_in, dkv_out, sems.at[1])]
+    for copy in copies:
+        copy.start()
+    for copy in copies:
+        copy.wait()
+
+
 def body(n, replicas, stash_q, stash_kv, upstream, lengths, domains, domain_weight):
     _, _, seq, q_cols = stash_q.shape
     kv_cols = stash_kv.shape[-1]
@@ -211,13 +228,15 @@
     chunks = q_cols // (min(CHUNK_HEADS, group) * HEAD_SIZE)
     dma = pltpu.SemaphoreType.DMA
     flops = 5 * 2 * seq * seq * q_cols
-    return pl.pallas_call(
+    args = [pltpu.with_memory_space_constraint(x, pltpu.HBM)
+            for x in (domain_weight, stash_q, stash_kv, upstream)]
+    results = pl.pallas_call(
         functools.partial(kernel, n, replicas),
         out_shape=(
             jax.ShapeDtypeStruct(stash_q.shape, stash_q.dtype),
             jax.ShapeDtypeStruct(stash_kv.shape, stash_kv.dtype),
         ),
-        in_specs=[pl.BlockSpec(memory_space=pltpu.SMEM)] * 3 + [pl.BlockSpec(memory_space=pltpu.HBM)] * 3,
+        in_specs=[pl.BlockSpec(memory_space=pl.ANY)] * 6,
         out_specs=[pl.BlockSpec(memory_space=pl.ANY)] * 2,
         scratch_shapes=[
             pltpu.VMEM((seq, q_cols), jnp.bfloat16),
@@ -226,6 +245,7 @@
             pltpu.VMEM((seq, q_cols), jnp.bfloat16),
             pltpu.VMEM((seq, kv_cols), jnp.bfloat16),
             pltpu.VMEM((replicas, 8, 128), jnp.int32),
+            pltpu.SMEM((1,), jnp.int32), pltpu.SMEM((1,), jnp.int32), pltpu.SMEM(domain_weight.shape, jnp.float32), dma((3,)),
             dma((chunks,)), dma((chunks,)), dma((chunks,)), dma((chunks,)),
             dma, dma, dma((replicas,)), dma((replicas,)),
             dma((chunks,)), dma((chunks,)), dma, dma,
@@ -234,7 +254,15 @@
             collective_id=0, has_side_effects=True, vmem_limit_bytes=24 * 1024 * 1024
         ),
         cost_estimate=pl.CostEstimate(flops=flops, bytes_accessed=4 * 2 * seq * q_cols, transcendentals=seq * q_cols),
-    )(lengths, domains, domain_weight, stash_q, stash_kv, upstream)
+    )(lengths, domains, *args)
+    results = [pltpu.with_memory_space_constraint(r, pltpu.VMEM) for r in results]
+    return pl.pallas_call(
+        store,
+        out_shape=tuple(jax.ShapeDtypeStruct(r.shape, r.dtype) for r in results),
+        in_specs=[pl.BlockSpec(memory_space=pl.ANY)] * 2,
+        out_specs=[pl.BlockSpec(memory_space=pl.ANY)] * 2,
+        scratch_shapes=[dma((2,))],
+    )(*results)
 
 
 def solution(mesh):

time: 44.8 us -> 40.4 us (0.902)
  local copies, waits for them, and re-layouts: 5.07 us -> 0 us
  Pallas kernels: 37.5 us -> 38.3 us
    unnamed x10 -> x0, local copies, waits for them, and re-layouts: 5.07 us -> none
    pallas_call x0 -> x1, Pallas kernels: none -> 1.07 us  [body(): pl.pallas_call(store, out_shape=tuple((jax.ShapeDtypeStruct(r.shape, r.dt...]
where the time goes in v2:
time: 40.4 us; the launch traced here: 40.2 us
  Pallas kernels  38.3 us (95%)
  between operations  1.93 us (5%)
    pallas_call x1, Pallas kernels, body(): pl.pallas_call(functools.partial(kernel, n, replicas), out_shape=(jax.Sha...  37.2 us
    pallas_call x1, Pallas kernels, body(): pl.pallas_call(store, out_shape=tuple((jax.ShapeDtypeStruct(r.shape, r.dt...  1.07 us

profile of v2, /device:TPU:0, one launch (start us, length us, event | category | flops | bytes accessed | tf_op | source)
XLA Modules:
  0.0 40.2 jit_solution(4045509267462904453)
XLA Ops:
  1.9 37.2 %shard_map.77 = (bf16[1,1,128,4096]{3,2,1,0:T(8,128)(2,1)S(1)}, bf16[1,1,128,1024]{3,2,1,0:T(8,128)(2,1)S(1)}) custom-call(s32[1]{0:T(128)S(6)} %copy.8.len_hbm, s32[1]{0:T(128)S(6)} %copy.9.dom_hbm, f32[7]{0:T(128)} %weight_hbm.1, bf16[1,1,128,4096]{3,2,1,0:T(8,128)(2,1)} %q_hbm.1, bf16[1,1,128,1024]{3,2,1,0:T(8,128)(2,1)} %kv_hbm.1, ...), custom_call_target="tpu_custom_call" | custom-call | flops 671088640 | bytes 4194304 | tf_op jit(solution)/shard_map/pallas_call | solution.py:233
  39.1 1.1 %shard_map.78 = (bf16[1,1,128,4096]{3,2,1,0:T(8,128)(2,1)}, bf16[1,1,128,1024]{3,2,1,0:T(8,128)(2,1)}) custom-call(bf16[1,1,128,4096]{3,2,1,0:T(8,128)(2,1)S(1)} %get-tuple-element.4.dq_in, bf16[1,1,128,1024]{3,2,1,0:T(8,128)(2,1)S(1)} %get-tuple-element.5.dkv_in), custom_call_target="tpu_custom_call" | custom-call | tf_op jit(solution)/shard_map/pallas_call | solution.py:259

commit v3 on v2

--- a/solution.py
+++ b/solution.py
@@ -12,6 +12,7 @@
 DOMAINS = 7
 MESH = pl.DeviceIdType.MESH
 CHUNK_HEADS = 4
+PACED_CHUNKS = 2
 NT = (((1,), (1,)), ((), ()))
 TN = (((0,), (0,)), ((), ()))
 
@@ -38,28 +39,15 @@
     g_to = base + lax.rem(place + half - 1, half)
     g_from = base + lax.rem(place + 1, half)
     crossed = place == half - 1
-
-    scalars = [
-        pltpu.make_async_copy(src, dst, scalar_sems.at[i])
-        for i, (src, dst) in enumerate(
-            ((len_hbm, len_ref), (dom_hbm, dom_ref), (weight_hbm, weight_ref)))
-    ]
-    for copy in scalars:
-        copy.start()
+    paced = (lax.rem(place, 2) == 1) & jnp.logical_not(crossed)
+    free = (lax.rem(place, 2) == 0) & jnp.logical_not(crossed)
+
     barrier = pltpu.get_barrier_semaphore()
     for other in (pair, g_to, g_from):
         pl.semaphore_signal(barrier, inc=1, device_id={"section": other}, device_id_type=MESH)
     for off in range(1, replicas):
         pl.semaphore_signal(barrier, inc=1, device_id={"dp": lax.rem(replica + off, replicas)},
                             device_id_type=MESH)
-
-    for copy in scalars:
-        copy.wait()
-    length = len_ref[0]
-    domain = dom_ref[0]
-    lane = lax.broadcasted_iota(jnp.int32, (8, 128), 1)
-    onehot = lane == domain
-    counts[0] = jnp.where(onehot, length, 0)
 
     def cols(c):
         return pl.ds(pl.multiple_of(c * width, width), width)
@@ -96,26 +84,43 @@
         for off in range(1, replicas)
     ]
 
+    scalars = [
+        pltpu.make_async_copy(src, dst, scalar_sems.at[i])
+        for i, (src, dst) in enumerate(
+            ((len_hbm, len_ref), (dom_hbm, dom_ref), (weight_hbm, weight_ref)))
+    ]
+    for copy in scalars:
+        copy.start()
+
+    pl.semaphore_wait(barrier, 3 + replicas - 1)
+
     @pl.when(crossed)
     def _():
         kv_local.start()
         for c in range(chunks):
             q_local(c).start()
 
-    pl.semaphore_wait(barrier, 3 + replicas - 1)
-
     @pl.when(jnp.logical_not(crossed))
     def _():
         kv_copy.start()
+
+    for c in range(chunks):
+        g_copy(c).start()
+
+        @pl.when(free | (paced & (c < 1)))
+        def _():
+            q_copy(c).start()
+
+    for copy in scalars:
+        copy.wait()
+    length = len_ref[0]
+    domain = dom_ref[0]
+    lane = lax.broadcasted_iota(jnp.int32, (8, 128), 1)
+    onehot = lane == domain
+    counts[0] = jnp.where(onehot, length, 0)
 
     for copy in count_copies:
         copy.start()
-    for c in range(chunks):
-        g_copy(c).start()
-
-        @pl.when(jnp.logical_not(crossed))
-        def _():
-            q_copy(c).start()
 
     weight = jnp.float32(0.0)
     for d in range(DOMAINS):
@@ -160,6 +165,16 @@
             @pl.when(jnp.logical_not(crossed))
             def _():
                 q_copy(c).wait_recv()
+                q_copy(c).wait_send()
+
+            @pl.when(paced & (c < PACED_CHUNKS - 1))
+            def _():
+                q_copy(c + 1).start()
+
+            @pl.when(paced & (c == PACED_CHUNKS - 1))
+            def _():
+                for later in range(PACED_CHUNKS, chunks):
+                    q_copy(later).start()
 
             for h in range(width // HEAD_SIZE):
                 at = pl.ds(pl.multiple_of(c * width + h * HEAD_SIZE, HEAD_SIZE), HEAD_SIZE)
@@ -205,7 +220,6 @@
         dkv_local.start()
         kv_copy.wait_send()
         for c in range(chunks):
-            q_copy(c).wait_send()
             dq_local(c).wait()
         dkv_local.wait()
 

time: 40.4 us -> 39.7 us (0.983)
  the two profiles are of different devices: /device:TPU:0 before, /device:TPU:1 now
where the time goes in v3:
time: 39.7 us; the launch traced here: 39.6 us
  Pallas kernels  37.6 us (95%)
  between operations  1.93 us (5%)
    pallas_call x1, Pallas kernels, body(): pl.pallas_call(functools.partial(kernel, n, replicas), out_shape=(jax.Sha...  36.6 us
    pallas_call x1, Pallas kernels, body(): pl.pallas_call(store, out_shape=tuple((jax.ShapeDtypeStruct(r.shape, r.dt...  1.07 us

profile of v3, /device:TPU:1, one launch (start us, length us, event | category | flops | bytes accessed | tf_op | source)
XLA Modules:
  0.0 39.6 jit_solution(8545237526226238800)
XLA Ops:
  1.9 36.6 %shard_map.77 = (bf16[1,1,128,4096]{3,2,1,0:T(8,128)(2,1)S(1)}, bf16[1,1,128,1024]{3,2,1,0:T(8,128)(2,1)S(1)}) custom-call(s32[1]{0:T(128)S(6)} %copy.8.len_hbm, s32[1]{0:T(128)S(6)} %copy.9.dom_hbm, f32[7]{0:T(128)} %weight_hbm.1, bf16[1,1,128,4096]{3,2,1,0:T(8,128)(2,1)} %q_hbm.1, bf16[1,1,128,1024]{3,2,1,0:T(8,128)(2,1)} %kv_hbm.1, ...), custom_call_target="tpu_custom_call" | custom-call | flops 671088640 | bytes 4194304 | tf_op jit(solution)/shard_map/pallas_call | solution.py:247
  38.5 1.1 %shard_map.78 = (bf16[1,1,128,4096]{3,2,1,0:T(8,128)(2,1)}, bf16[1,1,128,1024]{3,2,1,0:T(8,128)(2,1)}) custom-call(bf16[1,1,128,4096]{3,2,1,0:T(8,128)(2,1)S(1)} %get-tuple-element.4.dq_in, bf16[1,1,128,1024]{3,2,1,0:T(8,128)(2,1)S(1)} %get-tuple-element.5.dkv_in), custom_call_target="tpu_custom_call" | custom-call | tf_op jit(solution)/shard_map/pallas_call | solution.py:273
